TPU v7x, 512 devices: a whole 4x8x8 slice. The times are simulated.
512 devices in a mesh: src: 32 (over z_lo, x, core), tgt: 16 (over z_hi, y).
Axes of the slice: x: 4, y: 8, z: 8 (z_hi: 2, z_lo: 4; z = z_hi * 4 + z_lo), core: 2. Of those that a mesh axis runs over, the one named last changes fastest.
Arguments:
- src_embed: bfloat16 [8192, 1024], P('src', 'tgt'), as said below
- tgt_embed: bfloat16 [4096, 1024], P('tgt', 'src')
- src_near: int32 [8192, 16], P('src'), may hold values from 0 to 4095
- tgt_near: int32 [4096, 16], P('tgt'), may hold values from 0 to 8191
Outputs:
- margin: bfloat16 [8192, 4096], P('src', 'tgt')
- src_average: float32 [8192], P('src')
- tgt_average: float32 [4096], P('tgt')
Inputs may be any that keep to these rules, and one draw needn't show every extreme that they name: `src_embed`: every embedding is a sentence-specific multiple of one direction shared by both languages plus independent variation of comparable size, so that all cosines of the draw are positive.
All inputs are finite; a program needn't handle non-finite values.
Results may differ from a plain program's by a relative error of at most 0.001.
Values may be sent and summed in bfloat16 or wider, within the bound.
No kernel may reach another device: no remote copies, remote signals or barrier semaphores. Data moves between devices by JAX's collectives and lax.ppermute only.
A program may use at most 64 MiB of HBM per device.

v0:
```python
import jax
import jax.numpy as jnp
from jax import lax
from jax.sharding import PartitionSpec as P

EPSILON = 1e-06


def square_sums(values):
    wide = values.astype(jnp.float32)
    return jnp.sum(wide * wide, axis=1)


def local(src_embed, tgt_embed, src_near, tgt_near):
    src_index = lax.axis_index("src")
    tgt_index = lax.axis_index("tgt")
    source_rows = lax.all_gather(src_embed, "tgt", axis=1, tiled=True)
    src_count = source_rows.shape[0]
    tgt_count = tgt_embed.shape[0]
    near_count = src_near.shape[1]
    src_norm = jnp.sqrt(square_sums(source_rows) + EPSILON)
    contract = (((1,), (1,)), ((), ()))
    target_rows = lax.all_gather(tgt_embed, "src", axis=1, tiled=True)
    products = lax.dot_general(
        source_rows, target_rows, contract, preferred_element_type=jnp.float32
    )
    tgt_squares = square_sums(target_rows)
    tgt_norm = jnp.sqrt(tgt_squares + EPSILON)
    cosine_tile = products / (src_norm[:, None] * tgt_norm[None, :])
    local_targets = src_near - tgt_index * tgt_count
    local_sources = tgt_near - src_index * src_count
    target_iota = lax.broadcasted_iota(jnp.int32, (1, tgt_count), 1)
    source_iota = lax.broadcasted_iota(jnp.int32, (src_count, 1), 0)

    def add_neighbour(step, sums):
        row_sum, column_sum = sums
        wanted_target = lax.dynamic_slice_in_dim(local_targets, step, 1, 1)
        row_hits = wanted_target == target_iota
        row_sum = row_sum + jnp.sum(jnp.where(row_hits, cosine_tile, 0.0), axis=1)
        wanted_source = lax.dynamic_slice_in_dim(local_sources, step, 1, 1)
        column_hits = source_iota == wanted_source.reshape(1, tgt_count)
        column_sum = column_sum + jnp.sum(jnp.where(column_hits, cosine_tile, 0.0), axis=0)
        return (row_sum, column_sum)

    start_sums = (jnp.zeros((src_count,), jnp.float32), jnp.zeros((tgt_count,), jnp.float32))
    row_partial, column_partial = lax.fori_loop(0, near_count, add_neighbour, start_sums)
    src_average = lax.psum(row_partial, "tgt") / near_count
    tgt_average = lax.psum(column_partial, "src") / near_count
    margin = (cosine_tile / ((src_average[:, None] + tgt_average[None, :]) / 2.0)).astype(
        jnp.bfloat16
    )
    return (margin, src_average, tgt_average)


def solution(mesh):
    placed = (P("src", "tgt"), P("tgt", "src"), P("src", None), P("tgt", None))
    return jax.shard_map(
        local,
        mesh=mesh,
        in_specs=placed,
        out_specs=(P("src", "tgt"), P("src"), P("tgt")),
        check_vma=False,
    )
```

profile of v0, /device:TPU:8, one launch (start us, length us, event | category | flops | bytes accessed | tf_op | source)
XLA Modules:
  0.0 227.9 jit_solution(2381617098433261783)
XLA Ops:
  0.6 47.4 %all_gather.7 = bf16[256,1024]{0,1:T(8,128)(2,1)S(1)} all-gather(bf16[256,32]{0,1:T(8,128)(2,1)} %param.7), channel_id=1, replica_groups=mesh['src'=32,'tgt'=16] {'src'}, dimensions={1}, use_global_device_ids=true | all-gather | bytes 540672 | tf_op jit(solution)/shard_map/all_gather | solution.py:23
  48.0 0.0 copy-start
  48.0 0.2 multiply_reduce_fusion
  48.2 0.6 copy-done
  48.8 51.3 %all_gather.6 = bf16[256,1024]{0,1:T(8,128)(2,1)S(1)} all-gather(bf16[256,64]{0,1:T(8,128)(2,1)S(1)} %copy-done), channel_id=1, replica_groups=mesh['src'=32,'tgt'=16] {'tgt'}, dimensions={1}, use_global_device_ids=true | all-gather | bytes 557056 | tf_op jit(solution)/shard_map/all_gather | solution.py:17
  100.1 0.2 multiply_reduce_fusion.1
  100.2 0.0 copy-start.2
  100.2 0.3 multiply_divide_fusion
  100.6 0.0 copy-start.1
  100.6 0.4 copy-done.2
  101.0 0.3 copy-done.1
  101.3 4.0 %while.16 = (s32[]{:T(128)}, f32[256]{0:T(256)S(1)}, f32[256]{0:T(256)S(1)}, s32[256,16]{0,1:T(8,128)S(1)}, f32[256,256]{1,0:T(8,128)S(1)}, /*index=5*/s32[256,16]{0,1:T(8,128)S(1)}, s32[]{:T(128)}, s32[]{:T(128)}) while((s32[]{:T(128)}, f32[256]{0:T(256)S(1)}, f32[256]{0:T(256)S(1)}, s32[256,16]{0,1:T(8,128)S(1)}, ...), condition=%wide.region_5.6_spmd.clone, body=%wide.region_2.5_spmd.clone.sunk | while | flops 393731 | bytes 276583 | solution.py:46
  101.3 0.2 select_reduce_fusion.3
  101.6 0.2 select_reduce_fusion.3
  101.8 0.2 select_reduce_fusion.3
  102.1 0.2 select_reduce_fusion.3
  102.4 0.2 select_reduce_fusion.3
  102.6 0.2 select_reduce_fusion.3
  102.9 0.2 select_reduce_fusion.3
  103.1 0.2 select_reduce_fusion.3
  103.4 0.2 select_reduce_fusion.3
  103.6 0.2 select_reduce_fusion.3
  103.9 0.2 select_reduce_fusion.3
  104.1 0.2 select_reduce_fusion.3
  104.4 0.2 select_reduce_fusion.3
  104.6 0.2 select_reduce_fusion.3
  104.9 0.2 select_reduce_fusion.3
  105.1 0.2 select_reduce_fusion.3
  105.3 67.4 %psum.15 = f32[256]{0:T(256)S(1)} all-reduce(f32[256]{0:T(256)S(1)} %get-tuple-element.144), channel_id=1, replica_groups=mesh['src'=32,'tgt'=16] {'src'}, use_global_device_ids=true, to_apply=%region_7.8 | all-reduce | flops 256 | bytes 2048 | tf_op jit(solution)/shard_map/psum | solution.py:48
  172.7 0.0 copy-start.3
  172.7 54.4 %psum.14 = f32[256]{0:T(256)S(1)} all-reduce(f32[256]{0:T(256)S(1)} %get-tuple-element.143), channel_id=1, replica_groups=mesh['src'=32,'tgt'=16] {'tgt'}, use_global_device_ids=true, to_apply=%region_6.7 | all-reduce | flops 256 | bytes 2048 | tf_op jit(solution)/shard_map/psum | solution.py:47
  227.1 0.0 copy-start.4
  227.1 0.0 copy-done.3
  227.1 0.8 fusion.5
  227.9 0.0 copy-done.4
  (55 shorter events, 0.6 us)
Async XLA Ops:
  48.0 0.8 copy-start
  100.2 0.7 copy-start.2
  100.6 0.7 copy-start.1
  172.7 54.4 %copy-start.3 = (f32[256]{0:T(256)}, f32[256]{0:T(256)S(1)}, u32[]{:S(2)}) copy-start(f32[256]{0:T(256)S(1)} %broadcast_multiply_fusion) | copy-start | bytes 3076
  227.1 0.8 copy-start.4
where the time goes:
time: 228 us
  blocking collectives  220 us (96%)
  other arithmetic  4.33 us (2%)
    psum x1, blocking collectives, local(): tgt_average = lax.psum(column_partial, 'src') / near_count  67.4 us
    psum x1, blocking collectives, local(): src_average = lax.psum(row_partial, 'tgt') / near_count  54.4 us
    all_gather x1, blocking collectives, local(): source_rows = lax.all_gather(src_embed, 'tgt', axis=1, tiled=True)  51.3 us
    all_gather x1, blocking collectives, local(): target_rows = lax.all_gather(tgt_embed, 'src', axis=1, tiled=True)  47.4 us

commit v1 on v0

--- a/solution.py
+++ b/solution.py
@@ -45,7 +45,7 @@
     start_sums = (jnp.zeros((src_count,), jnp.float32), jnp.zeros((tgt_count,), jnp.float32))
     row_partial, column_partial = lax.fori_loop(0, near_count, add_neighbour, start_sums)
     src_average = lax.psum(row_partial, "tgt") / near_count
-    tgt_average = lax.psum(column_partial, "src") / near_count
+    tgt_average = jnp.sum(lax.all_gather(column_partial, "src"), axis=0) / near_count
     margin = (cosine_tile / ((src_average[:, None] + tgt_average[None, :]) / 2.0)).astype(
         jnp.bfloat16
     )

time: 228 us -> 199 us (0.87)
  the two profiles are of different devices: /device:TPU:8 before, /device:TPU:10 now
where the time goes in v1:
time: 199 us
  blocking collectives  191 us (96%)
  other arithmetic  4.39 us (2%)
    psum x1, blocking collectives, local(): src_average = lax.psum(row_partial, 'tgt') / near_count  54.4 us
    all_gather x1, blocking collectives, local(): source_rows = lax.all_gather(src_embed, 'tgt', axis=1, tiled=True)  51 us
    all_gather x1, blocking collectives, local(): lax.all_gather(column_partial, 'src')  42.9 us
    all_gather x1, blocking collectives, local(): target_rows = lax.all_gather(tgt_embed, 'src', axis=1, tiled=True)  42.8 us

profile of v1, /device:TPU:10, one launch (start us, length us, event | category | flops | bytes accessed | tf_op | source)
XLA Modules:
  0.0 198.7 jit_solution(6658642173173271684)
XLA Ops:
  0.6 42.8 %all_gather.13 = bf16[256,1024]{0,1:T(8,128)(2,1)S(1)} all-gather(bf16[256,32]{0,1:T(8,128)(2,1)} %param.7), channel_id=1, replica_groups=mesh['src'=32,'tgt'=16] {'src'}, dimensions={1}, use_global_device_ids=true | all-gather | bytes 540672 | tf_op jit(solution)/shard_map/all_gather | solution.py:23
  43.4 0.0 copy-start
  43.4 0.2 multiply_reduce_fusion
  43.6 0.6 copy-done
  44.2 51.0 %all_gather.12 = bf16[256,1024]{0,1:T(8,128)(2,1)S(1)} all-gather(bf16[256,64]{0,1:T(8,128)(2,1)S(1)} %copy-done), channel_id=1, replica_groups=mesh['src'=32,'tgt'=16] {'tgt'}, dimensions={1}, use_global_device_ids=true | all-gather | bytes 557056 | tf_op jit(solution)/shard_map/all_gather | solution.py:17
  95.2 0.2 multiply_reduce_fusion.1
  95.4 0.0 copy-start.2
  95.4 0.3 multiply_divide_fusion
  95.8 0.0 copy-start.1
  95.8 0.4 copy-done.2
  96.1 0.4 copy-done.1
  96.5 4.0 %while.16 = (s32[]{:T(128)}, f32[256]{0:T(256)S(1)}, f32[256]{0:T(256)S(1)}, s32[256,16]{0,1:T(8,128)S(1)}, f32[256,256]{1,0:T(8,128)S(1)}, /*index=5*/s32[256,16]{0,1:T(8,128)S(1)}, s32[]{:T(128)}, s32[]{:T(128)}) while((s32[]{:T(128)}, f32[256]{0:T(256)S(1)}, f32[256]{0:T(256)S(1)}, s32[256,16]{0,1:T(8,128)S(1)}, ...), condition=%wide.region_5.6_spmd.clone, body=%wide.region_2.5_spmd.clone.sunk | while | flops 393731 | bytes 276583 | solution.py:46
  96.5 0.2 select_reduce_fusion.3
  96.8 0.2 select_reduce_fusion.3
  97.0 0.2 select_reduce_fusion.3
  97.3 0.2 select_reduce_fusion.3
  97.5 0.2 select_reduce_fusion.3
  97.8 0.2 select_reduce_fusion.3
  98.0 0.2 select_reduce_fusion.3
  98.3 0.2 select_reduce_fusion.3
  98.5 0.2 select_reduce_fusion.3
  98.8 0.2 select_reduce_fusion.3
  99.0 0.2 select_reduce_fusion.3
  99.3 0.2 select_reduce_fusion.3
  99.5 0.2 select_reduce_fusion.3
  99.8 0.2 select_reduce_fusion.3
  100.0 0.2 select_reduce_fusion.3
  100.3 0.2 select_reduce_fusion.3
  100.5 42.9 %all-gather.1 = f32[32,1,256]{2,1,0:T(1,128)S(1)} all-gather(f32[1,1,256]{2,1,0:T(1,128)S(1)} %bitcast.11), channel_id=2, replica_groups=mesh['src'=32,'tgt'=16] {'src'}, dimensions={0}, use_global_device_ids=true | all-gather | bytes 33792 | tf_op jit(solution)/shard_map/all_gather | solution.py:48
  143.5 0.1 reduce_sum.55
  143.5 0.0 copy-start.3
  143.5 54.4 %psum.7 = f32[256]{0:T(256)S(1)} all-reduce(f32[256]{0:T(256)S(1)} %get-tuple-element.143), channel_id=1, replica_groups=mesh['src'=32,'tgt'=16] {'tgt'}, use_global_device_ids=true, to_apply=%region_6.7 | all-reduce | flops 256 | bytes 2048 | tf_op jit(solution)/shard_map/psum | solution.py:47
  197.9 0.0 copy-start.4
  197.9 0.0 copy-done.3
  197.9 0.8 fusion.5
  198.7 0.0 copy-done.4
  (55 shorter events, 0.6 us)
Async XLA Ops:
  43.4 0.8 copy-start
  95.4 0.7 copy-start.2
  95.8 0.7 copy-start.1
  143.5 54.4 %copy-start.3 = (f32[256]{0:T(256)}, f32[256]{0:T(256)S(1)}, u32[]{:S(2)}) copy-start(f32[256]{0:T(256)S(1)} %broadcast_multiply_fusion) | copy-start | bytes 3076
  197.9 0.8 copy-start.4

commit v2 on v0

--- a/solution.py
+++ b/solution.py
@@ -14,7 +14,9 @@
 def local(src_embed, tgt_embed, src_near, tgt_near):
     src_index = lax.axis_index("src")
     tgt_index = lax.axis_index("tgt")
-    source_rows = lax.all_gather(src_embed, "tgt", axis=1, tiled=True)
+    source_rows = jnp.concatenate(
+        lax.all_to_all(jnp.stack([src_embed] * lax.axis_size("tgt")), "tgt", 0, 0), axis=1
+    )
     src_count = source_rows.shape[0]
     tgt_count = tgt_embed.shape[0]
     near_count = src_near.shape[1]

time: 228 us -> 190 us (0.83)
  the two profiles are of different devices: /device:TPU:8 before, /device:TPU:0 now
where the time goes in v2:
time: 190 us
  blocking collectives  171 us (90%)
  starting transfers between devices  10.3 us (5%)
  other arithmetic  4.33 us (2%)
  local copies, waits for them, and re-layouts  3.19 us (2%)
    psum x1, blocking collectives, local(): tgt_average = lax.psum(column_partial, 'src') / near_count  67.7 us
    psum x1, blocking collectives, local(): src_average = lax.psum(row_partial, 'tgt') / near_count  56.1 us
    all_gather x1, blocking collectives, local(): target_rows = lax.all_gather(tgt_embed, 'src', axis=1, tiled=True)  46.7 us
    all_to_all x1, starting transfers between devices, local(): lax.all_to_all(jnp.stack([src_embed] * lax.axis_size('tgt')), 'tgt', 0, 0)  10.3 us
  transfers between devices with their start and end apart: 1, of which 0 were waited for; matrix products, arithmetic and copies ran while one was open for 0% of the time, Pallas kernels for 0%

profile of v2, /device:TPU:0, one launch (start us, length us, event | category | flops | bytes accessed | tf_op | source)
XLA Modules:
  0.0 189.9 jit_solution(9432345069644469771)
XLA Ops:
  0.6 1.6 stack.2
  2.2 10.3 %all-to-all-start = ((bf16[16,256,64]{1,2,0:T(8,128)(2,1)}), bf16[16,256,64]{1,2,0:T(8,128)(2,1)S(1)}, u32[]{:S(2)}, u32[]{:S(2)}) async-start(bf16[16,256,64]{1,2,0:T(8,128)(2,1)} %stack.2), calls=%async_computation | async-start | bytes 1048576 | tf_op jit(solution)/shard_map/all_to_all | solution.py:18
  12.5 0.0 copy-start
  12.6 0.7 copy-done
  13.2 46.7 %all_gather.3 = bf16[256,1024]{0,1:T(8,128)(2,1)S(1)} all-gather(bf16[256,32]{0,1:T(8,128)(2,1)S(1)} %copy-done), channel_id=1, replica_groups=mesh['src'=32,'tgt'=16] {'src'}, dimensions={1}, use_global_device_ids=true | all-gather | bytes 540672 | tf_op jit(solution)/shard_map/all_gather | solution.py:25
  59.9 0.0 copy-start.1
  59.9 0.0 copy-start.2
  59.9 0.2 multiply_reduce_fusion
  60.1 0.5 copy-done.1
  60.6 0.0 copy-done.2
  60.7 0.0 all-to-all-done
  60.7 0.2 multiply_reduce_fusion.1
  60.8 0.3 multiply_divide_fusion
  61.2 4.0 %while.16 = (s32[]{:T(128)}, f32[256]{0:T(256)S(1)}, f32[256]{0:T(256)S(1)}, s32[256,16]{0,1:T(8,128)S(1)}, f32[256,256]{1,0:T(8,128)S(1)}, /*index=5*/s32[256,16]{0,1:T(8,128)S(1)}, s32[]{:T(128)}, s32[]{:T(128)}) while((s32[]{:T(128)}, f32[256]{0:T(256)S(1)}, f32[256]{0:T(256)S(1)}, s32[256,16]{0,1:T(8,128)S(1)}, ...), condition=%wide.region_5.6_spmd.clone, body=%wide.region_2.5_spmd.clone.sunk | while | flops 393731 | bytes 276583 | solution.py:48
  61.2 0.2 select_reduce_fusion.3
  61.5 0.2 select_reduce_fusion.3
  61.7 0.2 select_reduce_fusion.3
  62.0 0.2 select_reduce_fusion.3
  62.2 0.2 select_reduce_fusion.3
  62.5 0.2 select_reduce_fusion.3
  62.8 0.2 select_reduce_fusion.3
  63.0 0.2 select_reduce_fusion.3
  63.3 0.2 select_reduce_fusion.3
  63.5 0.2 select_reduce_fusion.3
  63.8 0.2 select_reduce_fusion.3
  64.0 0.2 select_reduce_fusion.3
  64.3 0.2 select_reduce_fusion.3
  64.5 0.2 select_reduce_fusion.3
  64.8 0.2 select_reduce_fusion.3
  65.0 0.2 select_reduce_fusion.3
  65.2 67.7 %psum.15 = f32[256]{0:T(256)S(1)} all-reduce(f32[256]{0:T(256)S(1)} %get-tuple-element.144), channel_id=1, replica_groups=mesh['src'=32,'tgt'=16] {'src'}, use_global_device_ids=true, to_apply=%region_7.8 | all-reduce | flops 256 | bytes 2048 | tf_op jit(solution)/shard_map/psum | solution.py:50
  133.0 0.0 copy-start.3
  133.0 56.1 %psum.14 = f32[256]{0:T(256)S(1)} all-reduce(f32[256]{0:T(256)S(1)} %get-tuple-element.143), channel_id=1, replica_groups=mesh['src'=32,'tgt'=16] {'tgt'}, use_global_device_ids=true, to_apply=%region_6.7 | all-reduce | flops 256 | bytes 2048 | tf_op jit(solution)/shard_map/psum | solution.py:49
  189.1 0.0 copy-start.4
  189.1 0.0 copy-done.3
  189.1 0.8 fusion.5
  189.9 0.0 copy-done.4
  (55 shorter events, 0.6 us)
Async XLA Ops:
  2.2 58.4 %all-to-all-start = ((bf16[16,256,64]{1,2,0:T(8,128)(2,1)}), bf16[16,256,64]{1,2,0:T(8,128)(2,1)S(1)}, u32[]{:S(2)}, u32[]{:S(2)}) async-start(bf16[16,256,64]{1,2,0:T(8,128)(2,1)} %stack.2), calls=%async_computation | async-start | bytes 1048576 | tf_op jit(solution)/shard_map/all_to_all | solution.py:18
  12.5 0.7 copy-start
  59.9 0.7 copy-start.1
  59.9 0.7 copy-start.2
  133.0 56.1 %copy-start.3 = (f32[256]{0:T(256)}, f32[256]{0:T(256)S(1)}, u32[]{:S(2)}) copy-start(f32[256]{0:T(256)S(1)} %broadcast_multiply_fusion) | copy-start | bytes 3076
  189.1 0.8 copy-start.4
